TPU v7x, 512 devices: a whole 4x4x16 slice. The times are simulated.
512 devices in a mesh: row: 32 (over y, x, core), col: 16 (over z).
Axes of the slice: x: 4, y: 4, z: 16, core: 2. Of those that a mesh axis runs over, the one named last changes fastest.
Arguments:
- matrix: float32 [12288, 12288], P('row', 'col'), may hold values from -10 to 10, as said below
- panel: float32 [12288, 64], P('row'), may hold values from -1.12763724 to 1.12763724
Outputs:
- updated: float32 [12288, 12288], P('row', 'col')
- band_block: float32 [64, 64], replicated
Inputs may be any that keep to these rules, and one draw needn't show every extreme that they name: matrix is exactly symmetric.
All inputs are finite; a program needn't handle non-finite values.
Results may differ from a plain program's by a relative error of at most 0.0002.
Values sent between devices are 32-bit elements; how exact they have to be, the bound alone decides.
A program may use at most 64 MiB of HBM per device.

v0:
```python
import jax
import jax.numpy as jnp
from jax import lax
from jax.sharding import PartitionSpec as P

precise = lax.Precision.HIGHEST


def partner_2(block, axis, stride):
    count = lax.axis_size(axis)
    route = []
    for low in range(count):
        high = low | 1 << stride
        if high != low and high < count:
            route += [(low, high), (high, low)]
    return lax.ppermute(block, axis, route)


def from_root(value, axis, source):
    kept = jnp.where(lax.axis_index(axis) == source, value, 0).astype(value.dtype)
    return lax.psum(kept, axis)


def upper_cholesky(gram_block):
    order_now = gram_block.shape[0]
    positions = jnp.arange(order_now)

    def one_column(column_index, lower_part):
        gram_column = lax.dynamic_slice_in_dim(gram_block, column_index, 1, 1)[:, 0]
        lower_row = lax.dynamic_slice_in_dim(lower_part, column_index, 1, 0)[0]
        earlier = jnp.where(positions < column_index, lower_row, 0.0)
        reduced = gram_column - jnp.dot(lower_part, earlier, precision=precise)
        pivot_value = jnp.sum(jnp.where(positions == column_index, reduced, 0.0))
        diagonal_value = jnp.sqrt(pivot_value)
        new_column = jnp.where(positions > column_index, reduced / diagonal_value, 0.0) + jnp.where(
            positions == column_index, diagonal_value, 0.0
        )
        return jnp.where(positions[None, :] == column_index, new_column[:, None], lower_part)

    lower_part = lax.fori_loop(
        0, order_now, one_column, jnp.zeros((order_now, order_now), jnp.float32)
    )
    return lower_part.T


def upper_inverse(upper_block):
    order_now = upper_block.shape[0]
    positions = jnp.arange(order_now)

    def one_row(step_count, inverse_part):
        row_at = order_now - 1 - step_count
        upper_row = lax.dynamic_slice_in_dim(upper_block, row_at, 1, 0)[0]
        diagonal_value = jnp.sum(jnp.where(positions == row_at, upper_row, 0.0))
        beyond = jnp.where(positions > row_at, upper_row, 0.0)
        unit_row = jnp.where(positions == row_at, 1.0, 0.0)
        new_row = (unit_row - jnp.dot(beyond, inverse_part, precision=precise)) / diagonal_value
        return jnp.where(positions[:, None] == row_at, new_row[None, :], inverse_part)

    return lax.fori_loop(0, order_now, one_row, jnp.zeros((order_now, order_now), jnp.float32))


def small_factor(block_in):
    order_now = block_in.shape[0]
    positions = jnp.arange(order_now)

    def one_pivot(pivot_index, state_pair):
        working, lower_whole = state_pair
        pivot_column = lax.dynamic_slice_in_dim(working, pivot_index, 1, 1)[:, 0]
        pivot_row = lax.dynamic_slice_in_dim(working, pivot_index, 1, 0)[0]
        pivot_value = jnp.sum(jnp.where(positions == pivot_index, pivot_column, 0.0))
        multipliers = jnp.where(positions > pivot_index, pivot_column / pivot_value, 0.0)
        lower_whole = lower_whole + multipliers[:, None] * (
            positions[None, :] == pivot_index
        ).astype(jnp.float32)
        working = working - multipliers[:, None] * pivot_row[None, :]
        return (working, lower_whole)

    working, lower_whole = lax.fori_loop(
        0, order_now, one_pivot, (block_in, jnp.eye(order_now, dtype=jnp.float32))
    )
    return (lower_whole, jnp.triu(working))


def body(matrix, panel):
    local_rows, local_columns = matrix.shape
    panel_width = panel.shape[1]
    row_index = lax.axis_index("row")
    current_column_index = lax.axis_index("col")
    local_inner = jnp.dot(panel.T, panel, precision=precise)
    head_rows = panel[:panel_width]
    band_factor = -upper_cholesky(local_inner)
    levels = lax.axis_size("row").bit_length() - 1
    for bit_level in range(levels):
        partner = partner_2(band_factor, "row", bit_level)
        keeps_first = row_index >> bit_level & 1 == 0
        earlier_one = jnp.where(keeps_first, band_factor, partner)
        later_one = jnp.where(keeps_first, partner, band_factor)
        paired = jnp.dot(earlier_one.T, earlier_one, precision=precise) + jnp.dot(
            later_one.T, later_one, precision=precise
        )
        band_factor = -upper_cholesky(paired)
    head_rows = from_root(head_rows, "row", 0)
    factor_inverse = upper_inverse(band_factor)
    orthogonal_rows = jnp.dot(panel, factor_inverse, precision=precise)
    orthogonal_head = jnp.dot(head_rows, factor_inverse, precision=precise)
    identity = jnp.eye(panel_width, dtype=jnp.float32)
    lower_whole, upper_whole = small_factor(orthogonal_head - identity)
    global_rows = row_index * local_rows + jnp.arange(local_rows)
    unit_rows = (global_rows[:, None] == jnp.arange(panel_width)[None, :]).astype(jnp.float32)
    reflect_rows = jnp.dot(
        orthogonal_rows - unit_rows, upper_inverse(upper_whole), precision=precise
    )
    triangle = -jnp.dot(upper_whole, upper_inverse(lower_whole.T), precision=precise)
    gathered_reflect = lax.all_gather(reflect_rows, "row", axis=0, tiled=True)
    reflect_columns = lax.dynamic_slice_in_dim(
        gathered_reflect, current_column_index * local_columns, local_columns, 0
    )
    partial_product = lax.dot_general(
        matrix, reflect_rows, (((0,), (0,)), ((), ())), precision=precise
    )
    product = lax.psum(partial_product, "row")
    applied_cols = jnp.dot(product, triangle, precision=precise)
    inner_part = jnp.dot(reflect_columns.T, applied_cols, precision=precise)
    inner_total = lax.psum(inner_part, "col")
    coupling = jnp.dot(triangle.T, inner_total, precision=precise)
    corrected_cols = applied_cols - 0.5 * jnp.dot(reflect_columns, coupling, precision=precise)
    gathered_corrected = lax.all_gather(corrected_cols, "col", axis=0, tiled=True)
    corrected_rows = lax.dynamic_slice_in_dim(
        gathered_corrected, row_index * local_rows, local_rows, 0
    )
    left_factor = jnp.concatenate([reflect_rows, corrected_rows], 1)
    right_factor = jnp.concatenate([corrected_cols, reflect_columns], 1)
    updated = matrix - lax.dot_general(
        left_factor, right_factor, (((1,), (1,)), ((), ())), precision=precise
    )
    return (updated, band_factor)


def solution(mesh):
    return jax.shard_map(
        body,
        mesh=mesh,
        in_specs=(P("row", "col"), P("row", None)),
        out_specs=(P("row", "col"), P()),
        check_vma=False,
    )
```

profile of v0, /device:TPU:14, one launch (start us, length us, event | category | flops | bytes accessed | tf_op | source)
XLA Modules:
  0.0 1399.8 jit_solution(851780001571916975)
XLA Ops:
  8.5 101.3 %while.159 = (s32[]{:T(128)}, f32[64,64]{1,0:T(8,128)S(1)}, f32[64,64]{0,1:T(8,128)S(1)}, s32[]{:T(128)}, s32[]{:T(128)}) while((s32[]{:T(128)}, f32[64,64]{1,0:T(8,128)S(1)}, f32[64,64]{0,1:T(8,128)S(1)}, s32[]{:T(128)}, s32[]{:T(128)}) %tuple.367), condition=%wide.region_2.3_spmd.clone.clone, body=%wide.region_0.2_spmd.clone.clone.sunk | while | flops 62274 | bytes 102632 | solution.py:40
  109.8 1.9 collective-permute-start
  113.4 101.3 %while.160 = (s32[]{:T(128)}, f32[64,64]{1,0:T(8,128)S(1)}, f32[64,64]{0,1:T(8,128)S(1)}, s32[]{:T(128)}, s32[]{:T(128)}) while((s32[]{:T(128)}, f32[64,64]{1,0:T(8,128)S(1)}, f32[64,64]{0,1:T(8,128)S(1)}, s32[]{:T(128)}, s32[]{:T(128)}) %tuple.370), condition=%wide.region_5.6_spmd.clone.clone, body=%wide.region_3.5_spmd.clone.clone.sunk | while | flops 62274 | bytes 102632 | solution.py:40
  214.7 2.7 collective-permute-start.1
  217.5 3.0 collective-permute-done.1
  220.9 101.3 %while.161 = (s32[]{:T(128)}, f32[64,64]{1,0:T(8,128)S(1)}, f32[64,64]{0,1:T(8,128)S(1)}, s32[]{:T(128)}, s32[]{:T(128)}) while((s32[]{:T(128)}, f32[64,64]{1,0:T(8,128)S(1)}, f32[64,64]{0,1:T(8,128)S(1)}, s32[]{:T(128)}, s32[]{:T(128)}) %tuple.373), condition=%wide.region_8.9_spmd.clone.clone, body=%wide.region_6.8_spmd.clone.clone.sunk | while | flops 62274 | bytes 102632 | solution.py:40
  322.3 3.3 collective-permute-start.2
  325.6 4.0 collective-permute-done.2
  330.1 101.3 %while.162 = (s32[]{:T(128)}, f32[64,64]{1,0:T(8,128)S(1)}, f32[64,64]{0,1:T(8,128)S(1)}, s32[]{:T(128)}, s32[]{:T(128)}) while((s32[]{:T(128)}, f32[64,64]{1,0:T(8,128)S(1)}, f32[64,64]{0,1:T(8,128)S(1)}, s32[]{:T(128)}, s32[]{:T(128)}) %tuple.376), condition=%wide.region_11.12_spmd.clone.clone, body=%wide.region_9.11_spmd.clone.clone.sunk | while | flops 62274 | bytes 102632 | solution.py:40
  431.4 4.1 collective-permute-start.3
  435.5 1.8 collective-permute-done.3
  437.9 101.3 %while.163 = (s32[]{:T(128)}, f32[64,64]{1,0:T(8,128)S(1)}, f32[64,64]{0,1:T(8,128)S(1)}, s32[]{:T(128)}, s32[]{:T(128)}) while((s32[]{:T(128)}, f32[64,64]{1,0:T(8,128)S(1)}, f32[64,64]{0,1:T(8,128)S(1)}, s32[]{:T(128)}, s32[]{:T(128)}) %tuple.379), condition=%wide.region_14.15_spmd.clone.clone, body=%wide.region_12.14_spmd.clone.clone.sunk | while | flops 62274 | bytes 102632 | solution.py:40
  539.2 4.0 collective-permute-start.4
  543.3 102.9 %psum.21 = f32[64,64]{1,0:T(8,128)S(1)} all-reduce(f32[64,64]{1,0:T(8,128)S(1)} %broadcast_select_fusion.12), channel_id=1, replica_groups=mesh['row'=32,'col'=16] {'row'}, use_global_device_ids=true, to_apply=%region_21.22 | all-reduce | flops 4096 | bytes 32768 | tf_op jit(solution)/shard_map/psum | solution.py:21
  646.6 102.2 %while.164 = (s32[]{:T(128)}, f32[64,64]{1,0:T(8,128)S(1)}, f32[64,64]{0,1:T(8,128)S(1)}, s32[]{:T(128)}, s32[]{:T(128)}) while((s32[]{:T(128)}, f32[64,64]{1,0:T(8,128)S(1)}, f32[64,64]{0,1:T(8,128)S(1)}, s32[]{:T(128)}, s32[]{:T(128)}) %tuple.382), condition=%wide.region_17.18_spmd.clone.clone, body=%wide.region_15.17_spmd.clone.clone.sunk | while | flops 62274 | bytes 102632 | solution.py:40
  749.0 95.1 %while.165 = (s32[]{:T(128)}, f32[64,64]{1,0:T(8,128)S(1)}, f32[64,64]{1,0:T(8,128)S(1)}, s32[]{:T(128)}, s32[]{:T(128)}, /*index=5*/s32[]{:T(128)}, s32[]{:T(128)}) while((s32[]{:T(128)}, f32[64,64]{1,0:T(8,128)S(1)}, f32[64,64]{1,0:T(8,128)S(1)}, s32[]{:T(128)}, s32[]{:T(128)}, /*index=5*/s32[]{:T(128)}, ...), condition=%wide.region_20.21_spmd.clone.clone, body=%wide.region_18.20_spmd.clone.clone.sunk | while | flops 62086 | bytes 69153 | solution.py:59
  844.3 100.7 %while.158 = (s32[]{:T(128)}, f32[64,64]{0,1:T(8,128)S(1)}, f32[64,64]{0,1:T(8,128)S(1)}, s32[]{:T(128)}) while((s32[]{:T(128)}, f32[64,64]{0,1:T(8,128)S(1)}, f32[64,64]{0,1:T(8,128)S(1)}, s32[]{:T(128)}) %tuple.388), condition=%wide.region_24.25_spmd.clone.clone, body=%wide.region_22.24_spmd.clone.clone.sunk | while | flops 16897 | bytes 69965 | solution.py:78
  945.1 95.1 %while.166 = (s32[]{:T(128)}, f32[64,64]{1,0:T(8,128)S(1)}, f32[64,64]{1,0:T(8,128)S(1)}, s32[]{:T(128)}, s32[]{:T(128)}, /*index=5*/s32[]{:T(128)}, s32[]{:T(128)}) while((s32[]{:T(128)}, f32[64,64]{1,0:T(8,128)S(1)}, f32[64,64]{1,0:T(8,128)S(1)}, s32[]{:T(128)}, s32[]{:T(128)}, /*index=5*/s32[]{:T(128)}, ...), condition=%wide.region_27.28_spmd.clone.clone, body=%wide.region_25.27_spmd.clone.clone.sunk | while | flops 62086 | bytes 69153 | solution.py:59
  1043.2 103.2 %while.167 = (s32[]{:T(128)}, f32[64,64]{1,0:T(8,128)S(1)}, f32[64,64]{1,0:T(8,128)S(1)}, s32[]{:T(128)}, s32[]{:T(128)}, /*index=5*/s32[]{:T(128)}, s32[]{:T(128)}) while((s32[]{:T(128)}, f32[64,64]{1,0:T(8,128)S(1)}, f32[64,64]{1,0:T(8,128)S(1)}, s32[]{:T(128)}, s32[]{:T(128)}, /*index=5*/s32[]{:T(128)}, ...), condition=%wide.region_31.32_spmd.clone.clone, body=%wide.region_29.31_spmd.clone.clone.sunk | while | flops 62086 | bytes 69153 | solution.py:59
  1146.5 45.9 %all-reduce.2.cloned.1.call-done = f32[768,64]{0,1:T(8,128)} async-done(((f32[768,64]{0,1:T(8,128)}), f32[768,64]{0,1:T(8,128)}) %all-reduce.2.cloned.1.call-update) | async-done | bytes 196624 | tf_op jit(solution)/shard_map/psum | solution.py:121
  1193.7 62.0 %all-gather.3.cloned.1.call-done = f32[12288,64]{0,1:T(8,128)} async-done(((f32[384,64]{0,1:T(8,128)}), f32[12288,64]{0,1:T(8,128)}) %all-gather.3.cloned.1.call-update) | async-done | bytes 3145744 | tf_op jit(solution)/shard_map/all_gather | solution.py:114
  1256.9 56.9 %psum.23 = f32[64,64]{1,0:T(8,128)S(1)} all-reduce(f32[64,64]{1,0:T(8,128)S(1)} %fusion.157), channel_id=1, replica_groups=mesh['row'=32,'col'=16] {'col'}, use_global_device_ids=true, to_apply=%region_32.33 | all-reduce | flops 4096 | bytes 32768 | tf_op jit(solution)/shard_map/psum | solution.py:124
  1315.1 74.2 %all-gather.5.cloned.1.call-done = f32[12288,64]{0,1:T(8,128)} async-done(((f32[768,64]{0,1:T(8,128)}), f32[12288,64]{0,1:T(8,128)}) %all-gather.5.cloned.1.call-update) | async-done | bytes 3145744 | tf_op jit(solution)/shard_map/all_gather | solution.py:127
  1390.2 3.1 convolution_subtract_fusion
  (3080 shorter events, 738.7 us)
Async XLA Ops:
  7.2 104.6 %slice-start = ((f32[384,64]{0,1:T(8,128)}), f32[64,64]{0,1:T(8,128)S(1)}, s32[]{:S(2)}) async-start(f32[384,64]{0,1:T(8,128)} %param.23), calls=%async_computation.3 | async-start | bytes 65536 | tf_op jit(solution)/shard_map/slice | solution.py:90
  7.2 1185.2 %all-reduce.2.cloned.1.call-start = ((), (), s32[]{:S(2)}) async-start(), calls=%async_computation | async-start | bytes 393216 | tf_op jit(solution)/shard_map/psum | solution.py:121
  109.8 3.1 collective-permute-start
  214.7 5.8 collective-permute-start.1
  322.3 7.3 collective-permute-start.2
  431.4 6.0 collective-permute-start.3
  539.2 107.0 %collective-permute-start.4 = (f32[64,64]{0,1:T(8,128)S(1)}, f32[64,64]{0,1:T(8,128)S(1)}, u32[]{:S(2)}, u32[]{:S(2)}) collective-permute-start(f32[64,64]{0,1:T(8,128)S(1)} %negate_bitcast_fusion.1), channel_id=1, source_target_pairs={{0,256},{256,0},{16,272},{272,16},{32,288},{288,32},{48,304},{304,... | collective-permute-start | bytes 49160 | tf_op jit(solution)/shard_map/ppermute | solution.py:16
  748.9 291.3 %copy-start.3 = (f32[384,64]{0,1:T(8,128)S(1)}, f32[384,64]{0,1:T(8,128)}, u32[]{:S(2)}) copy-start(f32[384,64]{0,1:T(8,128)} %param.23) | copy-start | bytes 294916
  749.0 291.9 %copy-start = (f32[384,768]{1,0:T(8,128)S(1)}, f32[384,768]{1,0:T(8,128)}, u32[]{:S(2)}) copy-start(f32[384,768]{1,0:T(8,128)} %param.22) | copy-start | bytes 3538948
  844.1 196.8 %copy-start.4 = (f32[64,64]{1,0:T(8,128)}, f32[64,64]{1,0:T(8,128)S(1)}, u32[]{:S(2)}) copy-start(f32[64,64]{1,0:T(8,128)S(1)} %get-tuple-element.1720) | copy-start | bytes 49156
  1040.8 1.6 copy-start.1
  1042.4 213.3 %all-gather.3.cloned.1.call-start = ((), (), s32[]{:S(2)}) async-start(), calls=%async_computation.1 | async-start | bytes 3244032 | tf_op jit(solution)/shard_map/all_gather | solution.py:114
  1043.1 346.2 %all-gather.5.cloned.1.call-start = ((), (), s32[]{:S(2)}) async-start(), calls=%async_computation.2 | async-start | bytes 3342336 | tf_op jit(solution)/shard_map/all_gather | solution.py:127
  1146.5 243.7 %copy-start.2 = (f32[384,64]{0,1:T(8,128)S(1)}, f32[384,64]{0,1:T(8,128)}, u32[]{:S(2)}) copy-start(f32[384,64]{0,1:T(8,128)} %copy-done.1) | copy-start | bytes 294916
Sparse Core Ops, SparseCore 0:
  1042.5 149.8 all-reduce.1
  1196.1 59.4 all-gather.2
  1315.2 74.0 all-gather.4
where the time goes:
time: 1410 us; the launch traced here: 1400 us
  matrix products  464 us (33%)
  loops' own time  277 us (20%)
  other arithmetic  262 us (19%)
  waiting for transfers between devices  193 us (14%)
  blocking collectives  160 us (11%)
  starting transfers between devices  16.2 us (1%)
  between operations  14.2 us (1%)
    dot_general x384, matrix products, one_column(): reduced = gram_column - jnp.dot(lower_part, earlier, precision=precise)  299 us
    another operation x6, loops' own time, upper_cholesky(): lax.fori_loop(0, order_now, one_column, jnp.zeros((order_now, order_now),...  274 us
    dot_general x192, matrix products, one_row(): jnp.dot(beyond, inverse_part, precision=precise)  154 us
    reduce_sum x192, other arithmetic, one_row(): diagonal_value = jnp.sum(jnp.where(positions == row_at, upper_row, 0.0))  123 us
    psum x1, blocking collectives, from_root(): return lax.psum(kept, axis)  103 us
    all_gather x1, waiting for transfers between devices, body(): lax.all_gather(corrected_cols, 'col', axis=0, tiled=True)  74.2 us
    all_gather x1, waiting for transfers between devices, body(): gathered_reflect = lax.all_gather(reflect_rows, 'row', axis=0, tiled=True)  62 us
    psum x1, blocking collectives, body(): inner_total = lax.psum(inner_part, 'col')  56.9 us
  transfers between devices with their start and end apart: 8, of which 7 were waited for; matrix products, arithmetic and copies ran while one was open for 7% of the time, Pallas kernels for 0%

commit v1 on v0

--- a/solution.py
+++ b/solution.py
@@ -121,7 +121,11 @@
     product = lax.psum(partial_product, "row")
     applied_cols = jnp.dot(product, triangle, precision=precise)
     inner_part = jnp.dot(reflect_columns.T, applied_cols, precision=precise)
-    inner_total = lax.psum(inner_part, "col")
+    inner_total = inner_part
+    for hop in (1, 2, 4, 8):
+        inner_total = inner_total + lax.ppermute(
+            inner_total, "col", [(dev, dev ^ hop) for dev in range(16)]
+        )
     coupling = jnp.dot(triangle.T, inner_total, precision=precise)
     corrected_cols = applied_cols - 0.5 * jnp.dot(reflect_columns, coupling, precision=precise)
     gathered_corrected = lax.all_gather(corrected_cols, "col", axis=0, tiled=True)

time: 1410 us -> 1380 us (0.979)
  blocking collectives: 160 us -> 103 us
  starting transfers between devices: 16.2 us -> 45.8 us
  waiting for transfers between devices: 193 us -> 209 us
    psum x1 -> x0, blocking collectives: 56.9 us -> none  [body(): inner_total = lax.psum(inner_part, 'col')]
    ppermute x0 -> x4, starting transfers between devices: none -> 29.6 us  [body(): lax.ppermute(inner_total, 'col', [(dev, dev ^ hop) for dev in range(16)])]
  transfers between devices with their start and end apart: 8 -> 12, of which waited for: 7 -> 11; matrix products, arithmetic and copies ran while one was open for 7% -> 7% of each run, Pallas kernels for 0% -> 0%
where the time goes in v1:
time: 1380 us
  matrix products  458 us (33%)
  loops' own time  272 us (20%)
  other arithmetic  261 us (19%)
  waiting for transfers between devices  209 us (15%)
  blocking collectives  103 us (7%)
  starting transfers between devices  45.8 us (3%)
  between operations  14.3 us (1%)
  local copies, waits for them, and re-layouts  13.9 us (1%)
    dot_general x384, matrix products, one_column(): reduced = gram_column - jnp.dot(lower_part, earlier, precision=precise)  297 us
    another operation x6, loops' own time, upper_cholesky(): lax.fori_loop(0, order_now, one_column, jnp.zeros((order_now, order_now),...  269 us
    dot_general x192, matrix products, one_row(): jnp.dot(beyond, inverse_part, precision=precise)  150 us
    reduce_sum x192, other arithmetic, one_row(): diagonal_value = jnp.sum(jnp.where(positions == row_at, upper_row, 0.0))  122 us
    psum x1, blocking collectives, from_root(): return lax.psum(kept, axis)  103 us
    all_gather x1, waiting for transfers between devices, body(): lax.all_gather(corrected_cols, 'col', axis=0, tiled=True)  77.7 us
    all_gather x1, waiting for transfers between devices, body(): gathered_reflect = lax.all_gather(reflect_rows, 'row', axis=0, tiled=True)  62 us
    psum x1, waiting for transfers between devices, body(): product = lax.psum(partial_product, 'row')  50.3 us
  transfers between devices with their start and end apart: 12, of which 11 were waited for; matrix products, arithmetic and copies ran while one was open for 7% of the time, Pallas kernels for 0%

profile of v1, /device:TPU:14, one launch (start us, length us, event | category | flops | bytes accessed | tf_op | source)
XLA Modules:
  0.0 1377.6 jit_solution(17804076295393093456)
XLA Ops:
  8.5 101.3 %while.159 = (s32[]{:T(128)}, f32[64,64]{1,0:T(8,128)S(1)}, f32[64,64]{0,1:T(8,128)S(1)}, s32[]{:T(128)}, s32[]{:T(128)}) while((s32[]{:T(128)}, f32[64,64]{1,0:T(8,128)S(1)}, f32[64,64]{0,1:T(8,128)S(1)}, s32[]{:T(128)}, s32[]{:T(128)}) %tuple.367), condition=%wide.region_2.3_spmd.clone.clone, body=%wide.region_0.2_spmd.clone.clone.sunk | while | flops 62274 | bytes 102632 | solution.py:40
  113.4 101.3 %while.160 = (s32[]{:T(128)}, f32[64,64]{1,0:T(8,128)S(1)}, f32[64,64]{0,1:T(8,128)S(1)}, s32[]{:T(128)}, s32[]{:T(128)}) while((s32[]{:T(128)}, f32[64,64]{1,0:T(8,128)S(1)}, f32[64,64]{0,1:T(8,128)S(1)}, s32[]{:T(128)}, s32[]{:T(128)}) %tuple.370), condition=%wide.region_5.6_spmd.clone.clone, body=%wide.region_3.5_spmd.clone.clone.sunk | while | flops 62274 | bytes 102632 | solution.py:40
  217.5 3.0 collective-permute-done.1
  220.9 101.3 %while.161 = (s32[]{:T(128)}, f32[64,64]{1,0:T(8,128)S(1)}, f32[64,64]{0,1:T(8,128)S(1)}, s32[]{:T(128)}, s32[]{:T(128)}) while((s32[]{:T(128)}, f32[64,64]{1,0:T(8,128)S(1)}, f32[64,64]{0,1:T(8,128)S(1)}, s32[]{:T(128)}, s32[]{:T(128)}) %tuple.373), condition=%wide.region_8.9_spmd.clone.clone, body=%wide.region_6.8_spmd.clone.clone.sunk | while | flops 62274 | bytes 102632 | solution.py:40
  322.3 3.3 collective-permute-start.2
  325.6 4.0 collective-permute-done.2
  330.1 101.3 %while.162 = (s32[]{:T(128)}, f32[64,64]{1,0:T(8,128)S(1)}, f32[64,64]{0,1:T(8,128)S(1)}, s32[]{:T(128)}, s32[]{:T(128)}) while((s32[]{:T(128)}, f32[64,64]{1,0:T(8,128)S(1)}, f32[64,64]{0,1:T(8,128)S(1)}, s32[]{:T(128)}, s32[]{:T(128)}) %tuple.376), condition=%wide.region_11.12_spmd.clone.clone, body=%wide.region_9.11_spmd.clone.clone.sunk | while | flops 62274 | bytes 102632 | solution.py:40
  431.4 4.1 collective-permute-start.3
  437.9 101.3 %while.163 = (s32[]{:T(128)}, f32[64,64]{1,0:T(8,128)S(1)}, f32[64,64]{0,1:T(8,128)S(1)}, s32[]{:T(128)}, s32[]{:T(128)}) while((s32[]{:T(128)}, f32[64,64]{1,0:T(8,128)S(1)}, f32[64,64]{0,1:T(8,128)S(1)}, s32[]{:T(128)}, s32[]{:T(128)}) %tuple.379), condition=%wide.region_14.15_spmd.clone.clone, body=%wide.region_12.14_spmd.clone.clone.sunk | while | flops 62274 | bytes 102632 | solution.py:40
  539.2 4.0 collective-permute-start.4
  543.3 102.9 %psum.14 = f32[64,64]{1,0:T(8,128)S(1)} all-reduce(f32[64,64]{1,0:T(8,128)S(1)} %broadcast_select_fusion.12), channel_id=1, replica_groups=mesh['row'=32,'col'=16] {'row'}, use_global_device_ids=true, to_apply=%region_21.22 | all-reduce | flops 4096 | bytes 32768 | tf_op jit(solution)/shard_map/psum | solution.py:21
  646.6 95.3 %while.164 = (s32[]{:T(128)}, f32[64,64]{1,0:T(8,128)S(1)}, f32[64,64]{0,1:T(8,128)S(1)}, s32[]{:T(128)}, s32[]{:T(128)}) while((s32[]{:T(128)}, f32[64,64]{1,0:T(8,128)S(1)}, f32[64,64]{0,1:T(8,128)S(1)}, s32[]{:T(128)}, s32[]{:T(128)}) %tuple.382), condition=%wide.region_17.18_spmd.clone.clone, body=%wide.region_15.17_spmd.clone.clone.sunk | while | flops 62274 | bytes 102632 | solution.py:40
  742.0 95.1 %while.165 = (s32[]{:T(128)}, f32[64,64]{1,0:T(8,128)S(1)}, f32[64,64]{1,0:T(8,128)S(1)}, s32[]{:T(128)}, s32[]{:T(128)}, /*index=5*/s32[]{:T(128)}, s32[]{:T(128)}) while((s32[]{:T(128)}, f32[64,64]{1,0:T(8,128)S(1)}, f32[64,64]{1,0:T(8,128)S(1)}, s32[]{:T(128)}, s32[]{:T(128)}, /*index=5*/s32[]{:T(128)}, ...), condition=%wide.region_20.21_spmd.clone.clone, body=%wide.region_18.20_spmd.clone.clone.sunk | while | flops 62086 | bytes 69153 | solution.py:59
  837.4 100.7 %while.158 = (s32[]{:T(128)}, f32[64,64]{0,1:T(8,128)S(1)}, f32[64,64]{0,1:T(8,128)S(1)}, s32[]{:T(128)}) while((s32[]{:T(128)}, f32[64,64]{0,1:T(8,128)S(1)}, f32[64,64]{0,1:T(8,128)S(1)}, s32[]{:T(128)}) %tuple.388), condition=%wide.region_24.25_spmd.clone.clone, body=%wide.region_22.24_spmd.clone.clone.sunk | while | flops 16897 | bytes 69965 | solution.py:78
  938.2 95.1 %while.166 = (s32[]{:T(128)}, f32[64,64]{1,0:T(8,128)S(1)}, f32[64,64]{1,0:T(8,128)S(1)}, s32[]{:T(128)}, s32[]{:T(128)}, /*index=5*/s32[]{:T(128)}, s32[]{:T(128)}) while((s32[]{:T(128)}, f32[64,64]{1,0:T(8,128)S(1)}, f32[64,64]{1,0:T(8,128)S(1)}, s32[]{:T(128)}, s32[]{:T(128)}, /*index=5*/s32[]{:T(128)}, ...), condition=%wide.region_27.28_spmd.clone.clone, body=%wide.region_25.27_spmd.clone.clone.sunk | while | flops 62086 | bytes 69153 | solution.py:59
  1036.2 98.6 %while.167 = (s32[]{:T(128)}, f32[64,64]{1,0:T(8,128)S(1)}, f32[64,64]{1,0:T(8,128)S(1)}, s32[]{:T(128)}, s32[]{:T(128)}, /*index=5*/s32[]{:T(128)}, s32[]{:T(128)}) while((s32[]{:T(128)}, f32[64,64]{1,0:T(8,128)S(1)}, f32[64,64]{1,0:T(8,128)S(1)}, s32[]{:T(128)}, s32[]{:T(128)}, /*index=5*/s32[]{:T(128)}, ...), condition=%wide.region_31.32_spmd.clone.clone, body=%wide.region_29.31_spmd.clone.clone.sunk | while | flops 62086 | bytes 69153 | solution.py:59
  1135.1 50.3 %all-reduce.2.cloned.1.call-done = f32[768,64]{0,1:T(8,128)} async-done(((f32[768,64]{0,1:T(8,128)}), f32[768,64]{0,1:T(8,128)}) %all-reduce.2.cloned.1.call-update) | async-done | bytes 196624 | tf_op jit(solution)/shard_map/psum | solution.py:121
  1186.6 62.0 %all-gather.3.cloned.1.call-done = f32[12288,64]{0,1:T(8,128)} async-done(((f32[384,64]{0,1:T(8,128)}), f32[12288,64]{0,1:T(8,128)}) %all-gather.3.cloned.1.call-update) | async-done | bytes 3145744 | tf_op jit(solution)/shard_map/all_gather | solution.py:114
  1249.9 3.5 collective-permute-start.5
  1255.8 4.4 collective-permute-start.6
  1262.5 7.6 collective-permute-start.7
  1272.2 14.0 %collective-permute-start.8 = (f32[64,64]{1,0:T(8,128)S(1)}, f32[64,64]{1,0:T(8,128)S(1)}, u32[]{:S(2)}, u32[]{:S(2)}) collective-permute-start(f32[64,64]{1,0:T(8,128)S(1)} %add.361), channel_id=1, source_target_pairs={{0,8},{1,9},{2,10},{3,11},{4,12},{5,13},{6,14},{7,15},{8,0},{9,1},... | collective-permute-start | bytes 49160 | tf_op jit(solution)/shard_map/ppermute | solution.py:126
  1289.4 77.7 %all-gather.5.cloned.1.call-done = f32[12288,64]{0,1:T(8,128)} async-done(((f32[768,64]{0,1:T(8,128)}), f32[12288,64]{0,1:T(8,128)}) %all-gather.5.cloned.1.call-update) | async-done | bytes 3145744 | tf_op jit(solution)/shard_map/all_gather | solution.py:131
  1368.0 3.1 convolution_subtract_fusion
  (3090 shorter events, 747.1 us)
Async XLA Ops:
  7.2 104.6 %slice-start = ((f32[384,64]{0,1:T(8,128)}), f32[64,64]{0,1:T(8,128)S(1)}, s32[]{:S(2)}) async-start(f32[384,64]{0,1:T(8,128)} %param.23), calls=%async_computation.3 | async-start | bytes 65536 | tf_op jit(solution)/shard_map/slice | solution.py:90
  7.2 1178.1 %all-reduce.2.cloned.1.call-start = ((), (), s32[]{:S(2)}) async-start(), calls=%async_computation | async-start | bytes 393216 | tf_op jit(solution)/shard_map/psum | solution.py:121
  109.8 3.1 collective-permute-start
  214.7 5.8 collective-permute-start.1
  322.3 7.3 collective-permute-start.2
  431.4 6.0 collective-permute-start.3
  539.2 107.0 %collective-permute-start.4 = (f32[64,64]{0,1:T(8,128)S(1)}, f32[64,64]{0,1:T(8,128)S(1)}, u32[]{:S(2)}, u32[]{:S(2)}) collective-permute-start(f32[64,64]{0,1:T(8,128)S(1)} %negate_bitcast_fusion.1), channel_id=1, source_target_pairs={{0,256},{256,0},{16,272},{272,16},{32,288},{288,32},{48,304},{304,... | collective-permute-start | bytes 49160 | tf_op jit(solution)/shard_map/ppermute | solution.py:16
  742.0 291.3 %copy-start.3 = (f32[384,64]{0,1:T(8,128)S(1)}, f32[384,64]{0,1:T(8,128)}, u32[]{:S(2)}) copy-start(f32[384,64]{0,1:T(8,128)} %param.23) | copy-start | bytes 294916
  742.0 291.9 %copy-start = (f32[384,768]{1,0:T(8,128)S(1)}, f32[384,768]{1,0:T(8,128)}, u32[]{:S(2)}) copy-start(f32[384,768]{1,0:T(8,128)} %param.22) | copy-start | bytes 3538948
  837.1 196.8 %copy-start.4 = (f32[64,64]{1,0:T(8,128)}, f32[64,64]{1,0:T(8,128)S(1)}, u32[]{:S(2)}) copy-start(f32[64,64]{1,0:T(8,128)S(1)} %get-tuple-element.1724) | copy-start | bytes 49156
  1033.9 1.6 copy-start.1
  1035.4 213.2 %all-gather.3.cloned.1.call-start = ((), (), s32[]{:S(2)}) async-start(), calls=%async_computation.1 | async-start | bytes 3244032 | tf_op jit(solution)/shard_map/all_gather | solution.py:114
  1036.2 330.9 %all-gather.5.cloned.1.call-start = ((), (), s32[]{:S(2)}) async-start(), calls=%async_computation.2 | async-start | bytes 3342336 | tf_op jit(solution)/shard_map/all_gather | solution.py:131
  1186.6 181.4 %copy-start.2 = (f32[384,64]{0,1:T(8,128)S(1)}, f32[384,64]{0,1:T(8,128)}, u32[]{:S(2)}) copy-start(f32[384,64]{0,1:T(8,128)} %copy-done.1) | copy-start | bytes 294916
  1249.9 5.8 collective-permute-start.5
  1255.8 6.7 collective-permute-start.6
  1262.5 9.7 collective-permute-start.7
  1272.2 15.9 %collective-permute-start.8 = (f32[64,64]{1,0:T(8,128)S(1)}, f32[64,64]{1,0:T(8,128)S(1)}, u32[]{:S(2)}, u32[]{:S(2)}) collective-permute-start(f32[64,64]{1,0:T(8,128)S(1)} %add.361), channel_id=1, source_target_pairs={{0,8},{1,9},{2,10},{3,11},{4,12},{5,13},{6,14},{7,15},{8,0},{9,1},... | collective-permute-start | bytes 49160 | tf_op jit(solution)/shard_map/ppermute | solution.py:126
Sparse Core Ops, SparseCore 0:
  1035.5 149.7 all-reduce.1
  1189.1 59.5 all-gather.2
  1289.5 77.4 all-gather.4
